TPU v7x, 256 devices: a whole 4x4x8 slice. The times are simulated.
256 devices in a mesh: tensor: 8 (over y, core), context: 32 (over x, z).
Axes of the slice: x: 4, y: 4, z: 8, core: 2. Of those that a mesh axis runs over, the one named last changes fastest.
Arguments:
- normed_input: bfloat16 [128, 128, 3072], P('context', 'tensor'), may hold values from -6 to 6
- w_qkv: bfloat16 [3072, 3, 2048], P(None, None, 'tensor'), may hold values from -0.109375 to 0.109375
- queries: bfloat16 [16384, 2048], P('context', 'tensor'), may hold values from -9.4 to 9.4
- saved_keys: bfloat16 [16384, 2048], P('context', 'tensor'), may hold values from -9.4 to 9.4
- values: bfloat16 [16384, 2048], P('context', 'tensor'), may hold values from -6 to 6
- attn_out: bfloat16 [16384, 2048], P('context', 'tensor'), may hold values from -6 to 6
- grad_out: bfloat16 [16384, 2048], P('context', 'tensor'), may hold values from -6 to 6
- window_tiles: int32 [128, 24], replicated, may hold values from -1 to 127, as said below
Outputs:
- grad_input: bfloat16 [128, 128, 3072], P('context', 'tensor')
- grad_w: float32 [3072, 3, 2048], P('context', None, 'tensor')
Inputs may be any that keep to these rules, and one draw needn't show every extreme that they name: `window_tiles`: row t lists in increasing order the key tiles that query tile t attends to, then -1 in its remaining entries; t itself is always listed, and every listed tile k has |k // 8 - t // 8| <= 1.
All inputs are finite; a program needn't handle non-finite values.
Results may differ from a plain program's by a relative error of at most 0.024.
Values may be sent and summed in bfloat16 or wider, within the bound.
A program may use at most 128 MiB of HBM per device.

v0:
```python
import math

import jax
import jax.numpy as jnp
from jax import lax
from jax.sharding import PartitionSpec as P

D = 3072
HD = 128
TILE = 128
TILES_FRAME = 8


def passed_along(block, axis, distance):
    devices = range(lax.axis_size(axis))
    route = [((i - distance) % len(devices), i) for i in devices]
    return lax.ppermute(block, axis, route)


def tile_mask(window_rows, first_key, count_keys):
    key_ids = first_key + jnp.arange(count_keys, dtype=jnp.int32)
    allowed = jnp.any(window_rows[:, :, None] == key_ids[None, None, :], axis=1)
    return jnp.repeat(jnp.repeat(allowed, TILE, axis=0), TILE, axis=1)


def attend_block(query_blk, cot_blk, lse_blk, delta_blk, key_blk, value_blk, mask, scale):
    scores = (
        jnp.einsum("qhe,khe->hqk", query_blk, key_blk, preferred_element_type=jnp.float32) * scale
    )
    probs = jnp.where(mask[None], jnp.exp(scores - lse_blk[:, :, None]), 0.0)
    probs_b = probs.astype(jnp.bfloat16)
    grad_v = jnp.einsum("hqk,qhe->khe", probs_b, cot_blk, preferred_element_type=jnp.float32)
    dprobs = jnp.einsum("qhe,khe->hqk", cot_blk, value_blk, preferred_element_type=jnp.float32)
    dscores = (probs * (dprobs - delta_blk[:, :, None])).astype(jnp.bfloat16)
    grad_q = (
        jnp.einsum("hqk,khe->qhe", dscores, key_blk, preferred_element_type=jnp.float32) * scale
    )
    grad_k = (
        jnp.einsum("hqk,qhe->khe", dscores, query_blk, preferred_element_type=jnp.float32) * scale
    )
    return (grad_q, grad_k, grad_v)


def body(normed_input, w_qkv, queries, saved_keys, values, attn_out, grad_out, window_tiles):
    scale = 1.0 / math.sqrt(HD)
    ctx_count = lax.axis_size("context")
    my_index = lax.axis_index("context")
    rows, width = queries.shape
    heads_dev = width // HD
    tiles_dev = rows // TILE
    reach = (2 * TILES_FRAME + tiles_dev - 2) // tiles_dev
    visits = min(ctx_count, 2 * reach + 1)
    start_by = -reach % ctx_count
    home_by = (reach - visits + 1) % ctx_count
    input_full = lax.all_gather(normed_input, "tensor", axis=1, tiled=True)
    my_window = lax.dynamic_slice_in_dim(window_tiles, my_index * tiles_dev, tiles_dev, 0)
    query_h = queries.reshape(rows, heads_dev, HD)
    cot_h = grad_out.reshape(rows, heads_dev, HD)
    key_h = saved_keys.reshape(rows, heads_dev, HD)
    value_h = values.reshape(rows, heads_dev, HD)

    def fold_stats(step, keys_now, row_max, row_sum):
        source = (my_index + reach - step) % ctx_count
        mask = tile_mask(my_window, source * tiles_dev, tiles_dev)
        scores = (
            jnp.einsum("qhe,khe->hqk", query_h, keys_now, preferred_element_type=jnp.float32)
            * scale
        )
        masked = jnp.where(mask[None], scores, -1e30)
        new_max = jnp.maximum(row_max, jnp.max(masked, axis=2))
        new_sum = row_sum * jnp.exp(row_max - new_max) + jnp.sum(
            jnp.exp(masked - new_max[:, :, None]), axis=2
        )
        return (new_max, new_sum)

    stat_keys = passed_along(key_h, "context", start_by)

    def stat_turn(step, carry):
        keys_now, row_max, row_sum = carry
        row_max, row_sum = fold_stats(step, keys_now, row_max, row_sum)
        keys_now = passed_along(keys_now, "context", 1)
        return (keys_now, row_max, row_sum)

    stat_init = (
        stat_keys,
        jnp.full((heads_dev, rows), -1e30, jnp.float32),
        jnp.zeros((heads_dev, rows), jnp.float32),
    )
    keys_tail, max_tail, sum_tail = lax.fori_loop(0, visits - 1, stat_turn, stat_init)
    row_max, row_sum = fold_stats(visits - 1, keys_tail, max_tail, sum_tail)
    lse = row_max + jnp.log(row_sum)
    delta = jnp.sum(
        cot_h.astype(jnp.float32) * attn_out.reshape(rows, heads_dev, HD).astype(jnp.float32),
        axis=2,
    ).T
    zeros_grad = jnp.zeros((rows, heads_dev, HD), jnp.float32)
    keys_first, values_first = (key_h, value_h)
    keys_first, values_first = passed_along((key_h, value_h), "context", start_by)

    def key_work(step, keys_now, values_now):
        source = (my_index + reach - step) % ctx_count
        mask = tile_mask(my_window, source * tiles_dev, tiles_dev)
        return attend_block(query_h, cot_h, lse, delta, keys_now, values_now, mask, scale)

    def cycle_turn(step, carry):
        keys_now, values_now, dkeys_now, dvalues_now, dquery_acc = carry
        grad_q, grad_k, grad_v = key_work(step, keys_now, values_now)
        keys_now, values_now = passed_along((keys_now, values_now), "context", 1)
        dkeys_now, dvalues_now = (
            passed_along((dkeys_now + grad_k).astype(jnp.bfloat16), "context", 1).astype(
                jnp.float32
            ),
            passed_along((dvalues_now + grad_v).astype(jnp.bfloat16), "context", 1).astype(
                jnp.float32
            ),
        )
        return (keys_now, values_now, dkeys_now, dvalues_now, dquery_acc + grad_q)

    start_cycle = (keys_first, values_first, zeros_grad, zeros_grad, zeros_grad)
    keys_last, values_last, dkeys_last, dvalues_last, dquery_acc = lax.fori_loop(
        0, visits - 1, cycle_turn, start_cycle
    )
    grad_q, grad_k, grad_v = key_work(visits - 1, keys_last, values_last)
    grad_q = dquery_acc + grad_q
    grad_k = dkeys_last + grad_k
    grad_v = dvalues_last + grad_v
    grad_k, grad_v = (
        passed_along(grad_k.astype(jnp.bfloat16), "context", home_by).astype(grad_k.dtype),
        passed_along(grad_v.astype(jnp.bfloat16), "context", home_by).astype(grad_v.dtype),
    )
    grad_qkv = jnp.stack(
        [
            grad_q.reshape(rows, width).astype(jnp.bfloat16),
            grad_k.reshape(rows, width).astype(jnp.bfloat16),
            grad_v.reshape(rows, width).astype(jnp.bfloat16),
        ],
        axis=1,
    )
    flat_grad = grad_qkv.reshape(rows, 3 * width)
    flat_w = w_qkv.reshape(w_qkv.shape[0], 3 * width)
    partial_input = lax.dot_general(
        flat_grad, flat_w, (((1,), (1,)), ((), ())), preferred_element_type=jnp.float32
    )
    partial_input = partial_input.reshape(tiles_dev, TILE, w_qkv.shape[0])
    grad_input = lax.psum_scatter(
        partial_input.astype(jnp.bfloat16), "tensor", scatter_dimension=1, tiled=True
    )
    input_rows = input_full.reshape(rows, input_full.shape[2])
    term = lax.dot_general(
        input_rows, flat_grad, (((0,), (0,)), ((), ())), preferred_element_type=jnp.float32
    )
    grad_w = lax.psum_scatter(
        term.reshape(lax.axis_size("context") * (D // ctx_count), 3, width).astype(jnp.bfloat16),
        "context",
        scatter_dimension=0,
        tiled=True,
    ).astype(jnp.float32)
    return (grad_input, grad_w)


def solution(mesh):
    placed = (
        P("context", "tensor", None),
        P(None, None, "tensor"),
        P("context", "tensor"),
        P("context", "tensor"),
        P("context", "tensor"),
        P("context", "tensor"),
        P("context", "tensor"),
        P(),
    )
    return jax.shard_map(
        body,
        mesh=mesh,
        in_specs=placed,
        out_specs=(P("context", "tensor", None), P("context", None, "tensor")),
        check_vma=False,
    )
```

profile of v0, /device:TPU:2, one launch (start us, length us, event | category | flops | bytes accessed | tf_op | source)
XLA Modules:
  0.0 656.1 jit_solution(12273857223579629502)
XLA Ops:
  9.1 7.2 %collective-permute-start.6 = (bf16[512,2,128]{0,2,1:T(8,128)(2,1)S(1)}, bf16[512,2,128]{0,2,1:T(8,128)(2,1)S(1)}, u32[]{:S(2)}, u32[]{:S(2)}) collective-permute-start(bf16[512,2,128]{0,2,1:T(8,128)(2,1)S(1)} %bitcast.163), channel_id=1, source_target_pairs={{4,0},{5,1},{6,2},{7,3},{8,4},{9,5},{10,6},{11,7},{12,8},{13,9},{1... | collective-permute-start | bytes 786440 | tf_op jit(solution)/shard_map/ppermute | solution.py:17
  21.1 17.2 %collective-permute-done.5 = bf16[512,2,128]{0,2,1:T(8,128)(2,1)} collective-permute-done((bf16[512,2,128]{0,2,1:T(8,128)(2,1)}, bf16[512,2,128]{0,2,1:T(8,128)(2,1)}, u32[]{:S(2)}, u32[]{:S(2)}) %collective-permute-start.5) | collective-permute-done | bytes 262176 | tf_op jit(solution)/shard_map/ppermute | solution.py:17
  39.5 76.2 %while.44 = (s32[]{:T(128)}, bf16[512,2,128]{2,0,1:T(8,128)(2,1)S(1)}, f32[2,512]{1,0:T(2,128)S(1)}, f32[2,512]{1,0:T(2,128)S(1)}, s32[4,24]{1,0:T(4,128)S(1)}, ...) while((s32[]{:T(128)}, ...), condition=%wide.region_4.5_spmd.clone, body=%wide.region_0.4_spmd.clone.sunk | while | flops 137893632 | bytes 7140113 | solution.py:89
  43.6 4.9 collective-permute-done
  51.1 6.2 collective-permute-done
  59.1 6.8 %collective-permute-done = bf16[512,2,128]{2,0,1:T(8,128)(2,1)S(1)} collective-permute-done((bf16[512,2,128]{2,0,1:T(8,128)(2,1)S(1)}, bf16[512,2,128]{2,0,1:T(8,128)(2,1)S(1)}, u32[]{:S(2)}, u32[]{:S(2)}) %collective-permute-start) | collective-permute-done | bytes 262176 | tf_op jit(solution)/shard_map/while/body/eval_jaxpr/ppermute | solution.py:17
  67.6 6.8 %collective-permute-done = bf16[512,2,128]{2,0,1:T(8,128)(2,1)S(1)} collective-permute-done((bf16[512,2,128]{2,0,1:T(8,128)(2,1)S(1)}, bf16[512,2,128]{2,0,1:T(8,128)(2,1)S(1)}, u32[]{:S(2)}, u32[]{:S(2)}) %collective-permute-start) | collective-permute-done | bytes 262176 | tf_op jit(solution)/shard_map/while/body/eval_jaxpr/ppermute | solution.py:17
  76.2 7.9 %collective-permute-done = bf16[512,2,128]{2,0,1:T(8,128)(2,1)S(1)} collective-permute-done((bf16[512,2,128]{2,0,1:T(8,128)(2,1)S(1)}, bf16[512,2,128]{2,0,1:T(8,128)(2,1)S(1)}, u32[]{:S(2)}, u32[]{:S(2)}) %collective-permute-start) | collective-permute-done | bytes 262176 | tf_op jit(solution)/shard_map/while/body/eval_jaxpr/ppermute | solution.py:17
  85.9 9.1 %collective-permute-done = bf16[512,2,128]{2,0,1:T(8,128)(2,1)S(1)} collective-permute-done((bf16[512,2,128]{2,0,1:T(8,128)(2,1)S(1)}, bf16[512,2,128]{2,0,1:T(8,128)(2,1)S(1)}, u32[]{:S(2)}, u32[]{:S(2)}) %collective-permute-start) | collective-permute-done | bytes 262176 | tf_op jit(solution)/shard_map/while/body/eval_jaxpr/ppermute | solution.py:17
  96.8 9.0 %collective-permute-done = bf16[512,2,128]{2,0,1:T(8,128)(2,1)S(1)} collective-permute-done((bf16[512,2,128]{2,0,1:T(8,128)(2,1)S(1)}, bf16[512,2,128]{2,0,1:T(8,128)(2,1)S(1)}, u32[]{:S(2)}, u32[]{:S(2)}) %collective-permute-start) | collective-permute-done | bytes 262176 | tf_op jit(solution)/shard_map/while/body/eval_jaxpr/ppermute | solution.py:17
  107.5 8.1 %collective-permute-done = bf16[512,2,128]{2,0,1:T(8,128)(2,1)S(1)} collective-permute-done((bf16[512,2,128]{2,0,1:T(8,128)(2,1)S(1)}, bf16[512,2,128]{2,0,1:T(8,128)(2,1)S(1)}, u32[]{:S(2)}, u32[]{:S(2)}) %collective-permute-start) | collective-permute-done | bytes 262176 | tf_op jit(solution)/shard_map/while/body/eval_jaxpr/ppermute | solution.py:17
  117.7 222.7 %while.45 = (s32[]{:T(128)}, bf16[512,2,128]{2,0,1:T(8,128)(2,1)S(1)}, bf16[512,2,128]{2,0,1:T(8,128)(2,1)}, f32[512,2,128]{2,0,1:T(8,128)S(1)}, f32[512,2,128]{...) while((s32[]{:T(128)}, ...), condition=%wide.region_11.12_spmd.clone, body=%wide.region_9.11_spmd.clone.sunk | while | flops 676332288 | bytes 23868332 | solution.py:120
  153.5 8.5 %collective-permute-done.3 = bf16[512,2,128]{2,0,1:T(8,128)(2,1)} collective-permute-done((bf16[512,2,128]{2,0,1:T(8,128)(2,1)}, bf16[512,2,128]{2,0,1:T(8,128)(2,1)}, u32[]{:S(2)}, u32[]{:S(2)}) %collective-permute-start.3) | collective-permute-done | bytes 262176 | tf_op jit(solution)/shard_map/while/body/eval_jaxpr/ppermute | solution.py:17
  163.1 4.6 collective-permute-done.4
  177.2 11.6 %collective-permute-done.3 = bf16[512,2,128]{2,0,1:T(8,128)(2,1)} collective-permute-done((bf16[512,2,128]{2,0,1:T(8,128)(2,1)}, bf16[512,2,128]{2,0,1:T(8,128)(2,1)}, u32[]{:S(2)}, u32[]{:S(2)}) %collective-permute-start.3) | collective-permute-done | bytes 262176 | tf_op jit(solution)/shard_map/while/body/eval_jaxpr/ppermute | solution.py:17
  189.8 4.6 collective-permute-done.4
  203.4 13.2 %collective-permute-done.3 = bf16[512,2,128]{2,0,1:T(8,128)(2,1)} collective-permute-done((bf16[512,2,128]{2,0,1:T(8,128)(2,1)}, bf16[512,2,128]{2,0,1:T(8,128)(2,1)}, u32[]{:S(2)}, u32[]{:S(2)}) %collective-permute-start.3) | collective-permute-done | bytes 262176 | tf_op jit(solution)/shard_map/while/body/eval_jaxpr/ppermute | solution.py:17
  217.6 4.6 collective-permute-done.4
  231.2 14.3 %collective-permute-done.3 = bf16[512,2,128]{2,0,1:T(8,128)(2,1)} collective-permute-done((bf16[512,2,128]{2,0,1:T(8,128)(2,1)}, bf16[512,2,128]{2,0,1:T(8,128)(2,1)}, u32[]{:S(2)}, u32[]{:S(2)}) %collective-permute-start.3) | collective-permute-done | bytes 262176 | tf_op jit(solution)/shard_map/while/body/eval_jaxpr/ppermute | solution.py:17
  246.4 4.6 collective-permute-done.4
  260.9 14.6 %collective-permute-done.3 = bf16[512,2,128]{2,0,1:T(8,128)(2,1)} collective-permute-done((bf16[512,2,128]{2,0,1:T(8,128)(2,1)}, bf16[512,2,128]{2,0,1:T(8,128)(2,1)}, u32[]{:S(2)}, u32[]{:S(2)}) %collective-permute-start.3) | collective-permute-done | bytes 262176 | tf_op jit(solution)/shard_map/while/body/eval_jaxpr/ppermute | solution.py:17
  276.5 4.6 collective-permute-done.4
  290.1 16.3 %collective-permute-done.3 = bf16[512,2,128]{2,0,1:T(8,128)(2,1)} collective-permute-done((bf16[512,2,128]{2,0,1:T(8,128)(2,1)}, bf16[512,2,128]{2,0,1:T(8,128)(2,1)}, u32[]{:S(2)}, u32[]{:S(2)}) %collective-permute-start.3) | collective-permute-done | bytes 262176 | tf_op jit(solution)/shard_map/while/body/eval_jaxpr/ppermute | solution.py:17
  307.4 4.4 collective-permute-done.4
  320.9 14.6 %collective-permute-done.3 = bf16[512,2,128]{2,0,1:T(8,128)(2,1)} collective-permute-done((bf16[512,2,128]{2,0,1:T(8,128)(2,1)}, bf16[512,2,128]{2,0,1:T(8,128)(2,1)}, u32[]{:S(2)}, u32[]{:S(2)}) %collective-permute-start.3) | collective-permute-done | bytes 262176 | tf_op jit(solution)/shard_map/while/body/eval_jaxpr/ppermute | solution.py:17
  347.8 13.6 %collective-permute-start.8 = (bf16[512,2,128]{2,0,1:T(8,128)(2,1)S(1)}, bf16[512,2,128]{2,0,1:T(8,128)(2,1)S(1)}, u32[]{:S(2)}, u32[]{:S(2)}) collective-permute-start(bf16[512,2,128]{2,0,1:T(8,128)(2,1)S(1)} %add_convert_fusion), channel_id=1, source_target_pairs={{4,0},{5,1},{6,2},{7,3},{8,4},{9,5},{10,6},{11,7},{12,8},{13,9},{1... | collective-permute-start | bytes 786440 | tf_op jit(solution)/shard_map/ppermute | solution.py:17
  365.6 6.3 convolution_convert_fusion
  371.8 6.6 %copy.75 = bf16[3072,3,256]{2,0,1:T(8,128)(2,1)} copy(bf16[3072,3,256]{0,2,1:T(8,128)(2,1)} %bitcast.151) | data formatting | bytes 9437184 | tf_op jit(solution)/shard_map/convert_element_type | solution.py:153
  378.6 6.7 %copy.72 = bf16[3072,3,256]{0,2,1:T(8,128)(2,1)} copy(bf16[3072,3,256]{2,0,1:T(8,128)(2,1)} %param.13) | data formatting | bytes 9437184 | tf_op args[1]
  385.4 6.4 convolution_convert_fusion.1
  391.9 217.1 %reduce-scatter.5.cloned.1.call-done = bf16[96,3,256]{2,0,1:T(8,128)(2,1)} async-done(((bf16[3072,3,256]{2,0,1:T(8,128)(2,1)}), bf16[96,3,256]{2,0,1:T(8,128)(2,1)}) %reduce-scatter.5.cloned.1.call-update) | async-done | bytes 147472 | tf_op jit(solution)/shard_map/reduce_scatter | solution.py:152
  610.6 39.0 %reduce-scatter.3.cloned.1.call-done = bf16[4,16,3072]{2,1,0:T(8,128)(2,1)} async-done(((bf16[4,128,3072]{2,1,0:T(8,128)(2,1)}), bf16[4,16,3072]{2,1,0:T(8,128)(2,1)}) %reduce-scatter.3.cloned.1.call-update) | async-done | bytes 393232 | tf_op jit(solution)/shard_map/reduce_scatter | solution.py:145
  (355 shorter events, 140.7 us)
Async XLA Ops:
  7.2 358.4 %all-gather.2.cloned.1.call-start = ((), (), s32[]{:S(2)}) async-start(), calls=%async_computation.3 | async-start | bytes 3538944 | tf_op jit(solution)/shard_map/all_gather | solution.py:55
  7.9 601.0 %reduce-scatter.5.cloned.1.call-start = ((), (), s32[]{:S(2)}) async-start(), calls=%async_computation.4 | async-start | bytes 4866048 | tf_op jit(solution)/shard_map/reduce_scatter | solution.py:152
  9.1 107.8 %collective-permute-start.6 = (bf16[512,2,128]{0,2,1:T(8,128)(2,1)S(1)}, bf16[512,2,128]{0,2,1:T(8,128)(2,1)S(1)}, u32[]{:S(2)}, u32[]{:S(2)}) collective-permute-start(bf16[512,2,128]{0,2,1:T(8,128)(2,1)S(1)} %bitcast.163), channel_id=1, source_target_pairs={{4,0},{5,1},{6,2},{7,3},{8,4},{9,5},{10,6},{11,7},{12,8},{13,9},{1... | collective-permute-start | bytes 786440 | tf_op jit(solution)/shard_map/ppermute | solution.py:17
  18.1 20.2 %collective-permute-start.5 = (bf16[512,2,128]{0,2,1:T(8,128)(2,1)}, bf16[512,2,128]{0,2,1:T(8,128)(2,1)}, u32[]{:S(2)}, u32[]{:S(2)}) collective-permute-start(bf16[512,2,128]{0,2,1:T(8,128)(2,1)} %bitcast), channel_id=1, source_target_pairs={{4,0},{5,1},{6,2},{7,3},{8,4},{9,5},{10,6},{11,7},{12,8},{13,9},{1... | collective-permute-start | bytes 786440 | tf_op jit(solution)/shard_map/ppermute | solution.py:17
  118.6 22.4 %collective-permute-start.2 = (bf16[512,2,128]{2,0,1:T(8,128)(2,1)S(1)}, bf16[512,2,128]{2,0,1:T(8,128)(2,1)}, u32[]{:S(2)}, u32[]{:S(2)}) collective-permute-start(bf16[512,2,128]{2,0,1:T(8,128)(2,1)S(1)} %copy.125), channel_id=1, source_target_pairs={{31,0},{0,1},{1,2},{2,3},{3,4},{4,5},{5,6},{6,7},{7,8},{8,9},{9,10... | collective-permute-start | bytes 786440 | tf_op jit(solution)/shard_map/while/body/eval_jaxpr/ppermute | solution.py:17
  118.7 22.3 %collective-permute-start.1 = (bf16[512,2,128]{2,0,1:T(8,128)(2,1)S(1)}, bf16[512,2,128]{2,0,1:T(8,128)(2,1)S(1)}, u32[]{:S(2)}, u32[]{:S(2)}) collective-permute-start(bf16[512,2,128]{2,0,1:T(8,128)(2,1)S(1)} %copy.124), channel_id=1, source_target_pairs={{31,0},{0,1},{1,2},{2,3},{3,4},{4,5},{5,6},{6,7},{7,8},{8,9},{9,10... | collective-permute-start | bytes 786440 | tf_op jit(solution)/shard_map/while/body/eval_jaxpr/ppermute | solution.py:17
  142.0 27.5 %collective-permute-start.2 = (bf16[512,2,128]{2,0,1:T(8,128)(2,1)S(1)}, bf16[512,2,128]{2,0,1:T(8,128)(2,1)}, u32[]{:S(2)}, u32[]{:S(2)}) collective-permute-start(bf16[512,2,128]{2,0,1:T(8,128)(2,1)S(1)} %copy.125), channel_id=1, source_target_pairs={{31,0},{0,1},{1,2},{2,3},{3,4},{4,5},{5,6},{6,7},{7,8},{8,9},{9,10... | collective-permute-start | bytes 786440 | tf_op jit(solution)/shard_map/while/body/eval_jaxpr/ppermute | solution.py:17
  143.5 25.9 %collective-permute-start.1 = (bf16[512,2,128]{2,0,1:T(8,128)(2,1)S(1)}, bf16[512,2,128]{2,0,1:T(8,128)(2,1)S(1)}, u32[]{:S(2)}, u32[]{:S(2)}) collective-permute-start(bf16[512,2,128]{2,0,1:T(8,128)(2,1)S(1)} %copy.124), channel_id=1, source_target_pairs={{31,0},{0,1},{1,2},{2,3},{3,4},{4,5},{5,6},{6,7},{7,8},{8,9},{9,10... | collective-permute-start | bytes 786440 | tf_op jit(solution)/shard_map/while/body/eval_jaxpr/ppermute | solution.py:17
  170.4 25.8 %collective-permute-start.2 = (bf16[512,2,128]{2,0,1:T(8,128)(2,1)S(1)}, bf16[512,2,128]{2,0,1:T(8,128)(2,1)}, u32[]{:S(2)}, u32[]{:S(2)}) collective-permute-start(bf16[512,2,128]{2,0,1:T(8,128)(2,1)S(1)} %copy.125), channel_id=1, source_target_pairs={{31,0},{0,1},{1,2},{2,3},{3,4},{4,5},{5,6},{6,7},{7,8},{8,9},{9,10... | collective-permute-start | bytes 786440 | tf_op jit(solution)/shard_map/while/body/eval_jaxpr/ppermute | solution.py:17
  170.5 25.7 %collective-permute-start.1 = (bf16[512,2,128]{2,0,1:T(8,128)(2,1)S(1)}, bf16[512,2,128]{2,0,1:T(8,128)(2,1)S(1)}, u32[]{:S(2)}, u32[]{:S(2)}) collective-permute-start(bf16[512,2,128]{2,0,1:T(8,128)(2,1)S(1)} %copy.124), channel_id=1, source_target_pairs={{31,0},{0,1},{1,2},{2,3},{3,4},{4,5},{5,6},{6,7},{7,8},{8,9},{9,10... | collective-permute-start | bytes 786440 | tf_op jit(solution)/shard_map/while/body/eval_jaxpr/ppermute | solution.py:17
  176.4 18.0 %collective-permute-start.4 = (bf16[512,2,128]{2,0,1:T(8,128)(2,1)}, bf16[512,2,128]{2,0,1:T(8,128)(2,1)}, u32[]{:S(2)}, u32[]{:S(2)}) collective-permute-start(bf16[512,2,128]{2,0,1:T(8,128)(2,1)} %fusion.77), channel_id=1, source_target_pairs={{31,0},{0,1},{1,2},{2,3},{3,4},{4,5},{5,6},{6,7},{7,8},{8,9},{9,10... | collective-permute-start | bytes 786440 | tf_op jit(solution)/shard_map/while/body/eval_jaxpr/ppermute | solution.py:17
  197.1 26.8 %collective-permute-start.2 = (bf16[512,2,128]{2,0,1:T(8,128)(2,1)S(1)}, bf16[512,2,128]{2,0,1:T(8,128)(2,1)}, u32[]{:S(2)}, u32[]{:S(2)}) collective-permute-start(bf16[512,2,128]{2,0,1:T(8,128)(2,1)S(1)} %copy.125), channel_id=1, source_target_pairs={{31,0},{0,1},{1,2},{2,3},{3,4},{4,5},{5,6},{6,7},{7,8},{8,9},{9,10... | collective-permute-start | bytes 786440 | tf_op jit(solution)/shard_map/while/body/eval_jaxpr/ppermute | solution.py:17
  197.2 26.8 %collective-permute-start.1 = (bf16[512,2,128]{2,0,1:T(8,128)(2,1)S(1)}, bf16[512,2,128]{2,0,1:T(8,128)(2,1)S(1)}, u32[]{:S(2)}, u32[]{:S(2)}) collective-permute-start(bf16[512,2,128]{2,0,1:T(8,128)(2,1)S(1)} %copy.124), channel_id=1, source_target_pairs={{31,0},{0,1},{1,2},{2,3},{3,4},{4,5},{5,6},{6,7},{7,8},{8,9},{9,10... | collective-permute-start | bytes 786440 | tf_op jit(solution)/shard_map/while/body/eval_jaxpr/ppermute | solution.py:17
  202.9 19.3 %collective-permute-start.4 = (bf16[512,2,128]{2,0,1:T(8,128)(2,1)}, bf16[512,2,128]{2,0,1:T(8,128)(2,1)}, u32[]{:S(2)}, u32[]{:S(2)}) collective-permute-start(bf16[512,2,128]{2,0,1:T(8,128)(2,1)} %fusion.77), channel_id=1, source_target_pairs={{31,0},{0,1},{1,2},{2,3},{3,4},{4,5},{5,6},{6,7},{7,8},{8,9},{9,10... | collective-permute-start | bytes 786440 | tf_op jit(solution)/shard_map/while/body/eval_jaxpr/ppermute | solution.py:17
  224.9 27.9 %collective-permute-start.2 = (bf16[512,2,128]{2,0,1:T(8,128)(2,1)S(1)}, bf16[512,2,128]{2,0,1:T(8,128)(2,1)}, u32[]{:S(2)}, u32[]{:S(2)}) collective-permute-start(bf16[512,2,128]{2,0,1:T(8,128)(2,1)S(1)} %copy.125), channel_id=1, source_target_pairs={{31,0},{0,1},{1,2},{2,3},{3,4},{4,5},{5,6},{6,7},{7,8},{8,9},{9,10... | collective-permute-start | bytes 786440 | tf_op jit(solution)/shard_map/while/body/eval_jaxpr/ppermute | solution.py:17
  225.0 27.9 %collective-permute-start.1 = (bf16[512,2,128]{2,0,1:T(8,128)(2,1)S(1)}, bf16[512,2,128]{2,0,1:T(8,128)(2,1)S(1)}, u32[]{:S(2)}, u32[]{:S(2)}) collective-permute-start(bf16[512,2,128]{2,0,1:T(8,128)(2,1)S(1)} %copy.124), channel_id=1, source_target_pairs={{31,0},{0,1},{1,2},{2,3},{3,4},{4,5},{5,6},{6,7},{7,8},{8,9},{9,10... | collective-permute-start | bytes 786440 | tf_op jit(solution)/shard_map/while/body/eval_jaxpr/ppermute | solution.py:17
  230.7 20.4 %collective-permute-start.4 = (bf16[512,2,128]{2,0,1:T(8,128)(2,1)}, bf16[512,2,128]{2,0,1:T(8,128)(2,1)}, u32[]{:S(2)}, u32[]{:S(2)}) collective-permute-start(bf16[512,2,128]{2,0,1:T(8,128)(2,1)} %fusion.77), channel_id=1, source_target_pairs={{31,0},{0,1},{1,2},{2,3},{3,4},{4,5},{5,6},{6,7},{7,8},{8,9},{9,10... | collective-permute-start | bytes 786440 | tf_op jit(solution)/shard_map/while/body/eval_jaxpr/ppermute | solution.py:17
  253.8 29.1 %collective-permute-start.2 = (bf16[512,2,128]{2,0,1:T(8,128)(2,1)S(1)}, bf16[512,2,128]{2,0,1:T(8,128)(2,1)}, u32[]{:S(2)}, u32[]{:S(2)}) collective-permute-start(bf16[512,2,128]{2,0,1:T(8,128)(2,1)S(1)} %copy.125), channel_id=1, source_target_pairs={{31,0},{0,1},{1,2},{2,3},{3,4},{4,5},{5,6},{6,7},{7,8},{8,9},{9,10... | collective-permute-start | bytes 786440 | tf_op jit(solution)/shard_map/while/body/eval_jaxpr/ppermute | solution.py:17
  253.8 29.0 %collective-permute-start.1 = (bf16[512,2,128]{2,0,1:T(8,128)(2,1)S(1)}, bf16[512,2,128]{2,0,1:T(8,128)(2,1)S(1)}, u32[]{:S(2)}, u32[]{:S(2)}) collective-permute-start(bf16[512,2,128]{2,0,1:T(8,128)(2,1)S(1)} %copy.124), channel_id=1, source_target_pairs={{31,0},{0,1},{1,2},{2,3},{3,4},{4,5},{5,6},{6,7},{7,8},{8,9},{9,10... | collective-permute-start | bytes 786440 | tf_op jit(solution)/shard_map/while/body/eval_jaxpr/ppermute | solution.py:17
  258.3 17.2 %collective-permute-start.3 = (bf16[512,2,128]{2,0,1:T(8,128)(2,1)}, bf16[512,2,128]{2,0,1:T(8,128)(2,1)}, u32[]{:S(2)}, u32[]{:S(2)}) collective-permute-start(bf16[512,2,128]{2,0,1:T(8,128)(2,1)} %fusion.76), channel_id=1, source_target_pairs={{31,0},{0,1},{1,2},{2,3},{3,4},{4,5},{5,6},{6,7},{7,8},{8,9},{9,10... | collective-permute-start | bytes 786440 | tf_op jit(solution)/shard_map/while/body/eval_jaxpr/ppermute | solution.py:17
  259.6 21.5 %collective-permute-start.4 = (bf16[512,2,128]{2,0,1:T(8,128)(2,1)}, bf16[512,2,128]{2,0,1:T(8,128)(2,1)}, u32[]{:S(2)}, u32[]{:S(2)}) collective-permute-start(bf16[512,2,128]{2,0,1:T(8,128)(2,1)} %fusion.77), channel_id=1, source_target_pairs={{31,0},{0,1},{1,2},{2,3},{3,4},{4,5},{5,6},{6,7},{7,8},{8,9},{9,10... | collective-permute-start | bytes 786440 | tf_op jit(solution)/shard_map/while/body/eval_jaxpr/ppermute | solution.py:17
  283.8 29.8 %collective-permute-start.2 = (bf16[512,2,128]{2,0,1:T(8,128)(2,1)S(1)}, bf16[512,2,128]{2,0,1:T(8,128)(2,1)}, u32[]{:S(2)}, u32[]{:S(2)}) collective-permute-start(bf16[512,2,128]{2,0,1:T(8,128)(2,1)S(1)} %copy.125), channel_id=1, source_target_pairs={{31,0},{0,1},{1,2},{2,3},{3,4},{4,5},{5,6},{6,7},{7,8},{8,9},{9,10... | collective-permute-start | bytes 786440 | tf_op jit(solution)/shard_map/while/body/eval_jaxpr/ppermute | solution.py:17
  283.9 29.8 %collective-permute-start.1 = (bf16[512,2,128]{2,0,1:T(8,128)(2,1)S(1)}, bf16[512,2,128]{2,0,1:T(8,128)(2,1)S(1)}, u32[]{:S(2)}, u32[]{:S(2)}) collective-permute-start(bf16[512,2,128]{2,0,1:T(8,128)(2,1)S(1)} %copy.124), channel_id=1, source_target_pairs={{31,0},{0,1},{1,2},{2,3},{3,4},{4,5},{5,6},{6,7},{7,8},{8,9},{9,10... | collective-permute-start | bytes 786440 | tf_op jit(solution)/shard_map/while/body/eval_jaxpr/ppermute | solution.py:17
  288.3 18.1 %collective-permute-start.3 = (bf16[512,2,128]{2,0,1:T(8,128)(2,1)}, bf16[512,2,128]{2,0,1:T(8,128)(2,1)}, u32[]{:S(2)}, u32[]{:S(2)}) collective-permute-start(bf16[512,2,128]{2,0,1:T(8,128)(2,1)} %fusion.76), channel_id=1, source_target_pairs={{31,0},{0,1},{1,2},{2,3},{3,4},{4,5},{5,6},{6,7},{7,8},{8,9},{9,10... | collective-permute-start | bytes 786440 | tf_op jit(solution)/shard_map/while/body/eval_jaxpr/ppermute | solution.py:17
  289.6 22.3 %collective-permute-start.4 = (bf16[512,2,128]{2,0,1:T(8,128)(2,1)}, bf16[512,2,128]{2,0,1:T(8,128)(2,1)}, u32[]{:S(2)}, u32[]{:S(2)}) collective-permute-start(bf16[512,2,128]{2,0,1:T(8,128)(2,1)} %fusion.77), channel_id=1, source_target_pairs={{31,0},{0,1},{1,2},{2,3},{3,4},{4,5},{5,6},{6,7},{7,8},{8,9},{9,10... | collective-permute-start | bytes 786440 | tf_op jit(solution)/shard_map/while/body/eval_jaxpr/ppermute | solution.py:17
  314.6 25.8 %collective-permute-start.2 = (bf16[512,2,128]{2,0,1:T(8,128)(2,1)S(1)}, bf16[512,2,128]{2,0,1:T(8,128)(2,1)}, u32[]{:S(2)}, u32[]{:S(2)}) collective-permute-start(bf16[512,2,128]{2,0,1:T(8,128)(2,1)S(1)} %copy.125), channel_id=1, source_target_pairs={{31,0},{0,1},{1,2},{2,3},{3,4},{4,5},{5,6},{6,7},{7,8},{8,9},{9,10... | collective-permute-start | bytes 786440 | tf_op jit(solution)/shard_map/while/body/eval_jaxpr/ppermute | solution.py:17
  314.7 25.8 %collective-permute-start.1 = (bf16[512,2,128]{2,0,1:T(8,128)(2,1)S(1)}, bf16[512,2,128]{2,0,1:T(8,128)(2,1)S(1)}, u32[]{:S(2)}, u32[]{:S(2)}) collective-permute-start(bf16[512,2,128]{2,0,1:T(8,128)(2,1)S(1)} %copy.124), channel_id=1, source_target_pairs={{31,0},{0,1},{1,2},{2,3},{3,4},{4,5},{5,6},{6,7},{7,8},{8,9},{9,10... | collective-permute-start | bytes 786440 | tf_op jit(solution)/shard_map/while/body/eval_jaxpr/ppermute | solution.py:17
  319.1 16.3 %collective-permute-start.3 = (bf16[512,2,128]{2,0,1:T(8,128)(2,1)}, bf16[512,2,128]{2,0,1:T(8,128)(2,1)}, u32[]{:S(2)}, u32[]{:S(2)}) collective-permute-start(bf16[512,2,128]{2,0,1:T(8,128)(2,1)} %fusion.76), channel_id=1, source_target_pairs={{31,0},{0,1},{1,2},{2,3},{3,4},{4,5},{5,6},{6,7},{7,8},{8,9},{9,10... | collective-permute-start | bytes 786440 | tf_op jit(solution)/shard_map/while/body/eval_jaxpr/ppermute | solution.py:17
  320.4 18.2 %collective-permute-start.4 = (bf16[512,2,128]{2,0,1:T(8,128)(2,1)}, bf16[512,2,128]{2,0,1:T(8,128)(2,1)}, u32[]{:S(2)}, u32[]{:S(2)}) collective-permute-start(bf16[512,2,128]{2,0,1:T(8,128)(2,1)} %fusion.77), channel_id=1, source_target_pairs={{31,0},{0,1},{1,2},{2,3},{3,4},{4,5},{5,6},{6,7},{7,8},{8,9},{9,10... | collective-permute-start | bytes 786440 | tf_op jit(solution)/shard_map/while/body/eval_jaxpr/ppermute | solution.py:17
  344.1 17.9 %collective-permute-start.7 = (bf16[512,2,128]{2,0,1:T(8,128)(2,1)S(1)}, bf16[512,2,128]{2,0,1:T(8,128)(2,1)S(1)}, u32[]{:S(2)}, u32[]{:S(2)}) collective-permute-start(bf16[512,2,128]{2,0,1:T(8,128)(2,1)S(1)} %add_convert_fusion.1), channel_id=1, source_target_pairs={{4,0},{5,1},{6,2},{7,3},{8,4},{9,5},{10,6},{11,7},{12,8},{13,9},{1... | collective-permute-start | bytes 786440 | tf_op jit(solution)/shard_map/ppermute | solution.py:17
  347.8 17.5 %collective-permute-start.8 = (bf16[512,2,128]{2,0,1:T(8,128)(2,1)S(1)}, bf16[512,2,128]{2,0,1:T(8,128)(2,1)S(1)}, u32[]{:S(2)}, u32[]{:S(2)}) collective-permute-start(bf16[512,2,128]{2,0,1:T(8,128)(2,1)S(1)} %add_convert_fusion), channel_id=1, source_target_pairs={{4,0},{5,1},{6,2},{7,3},{8,4},{9,5},{10,6},{11,7},{12,8},{13,9},{1... | collective-permute-start | bytes 786440 | tf_op jit(solution)/shard_map/ppermute | solution.py:17
  378.5 271.1 %reduce-scatter.3.cloned.1.call-start = ((), (), s32[]{:S(2)}) async-start(), calls=%async_computation.2 | async-start | bytes 3538944 | tf_op jit(solution)/shard_map/reduce_scatter | solution.py:145
  (32 other events, 348.2 us)
Sparse Core Ops, SparseCore 0:
  9.9 33.2 all-gather.1
  378.6 230.2 reduce-scatter.4
  612.1 37.4 reduce-scatter.2
where the time goes:
time: 657 us; the launch traced here: 656 us
  waiting for transfers between devices  467 us (71%)
  matrix products  54.3 us (8%)
  local copies, waits for them, and re-layouts  45.3 us (7%)
  starting transfers between devices  41.2 us (6%)
  other arithmetic  32.5 us (5%)
  between operations  14.1 us (2%)
    reduce_scatter x1, waiting for transfers between devices, body(): lax.psum_scatter(term.reshape(lax.axis_size('context') * (D // ctx_count)...  217 us
    ppermute x44, waiting for transfers between devices, passed_along(): return lax.ppermute(block, axis, route)  210 us
    ppermute x44, starting transfers between devices, passed_along(): return lax.ppermute(block, axis, route)  41 us
    reduce_scatter x1, waiting for transfers between devices, body(): lax.psum_scatter(partial_input.astype(jnp.bfloat16), 'tensor', scatter_di...  39 us
    convert_element_type x8, other arithmetic, cycle_turn(): passed_along((dvalues_now + grad_v).astype(jnp.bfloat16), 'context', 1)  14.2 us
    broadcast_in_dim x25, local copies, waits for them, and re-layouts, tile_mask(): return jnp.repeat(jnp.repeat(allowed, TILE, axis=0), TILE, axis=1)  13.7 us
    unnamed x32, local copies, waits for them, and re-layouts  13.5 us
  transfers between devices with their start and end apart: 47, of which 28 were waited for; matrix products, arithmetic and copies ran while one was open for 18% of the time, Pallas kernels for 0%

commit v1 on v0

v1 whole, which is shorter than its diff:
```python
import functools
import math

import jax
import jax.numpy as jnp
from jax import lax
from jax.experimental import pallas as pl
from jax.experimental.pallas import tpu as pltpu
from jax.sharding import PartitionSpec as P

D = 3072
HD = 128
TILE = 128
NX, NZ, NY, NK = 4, 8, 4, 2
NT, NC = NY * NK, NX * NZ
HEADS = 2
WIDTH = HEADS * HD
TILES = 4
ROWS = TILES * TILE
QUERIES = 2 * ROWS
SLOTS = 3
KEYS = SLOTS * ROWS
SHARE = TILE // NT
DX = D // NX
DZ = DX // NZ
CHUNK = 256
SCALE = 1.0 / math.sqrt(HD)
LOG2E = 1.4426950408889634
MASKED = -1e30
MESH = pl.DeviceIdType.MESH
NN = (((1,), (0,)), ((), ()))
NTR = (((1,), (1,)), ((), ()))
F32 = jnp.float32
BF16 = jnp.bfloat16


def dot(a, b, dims):
    return lax.dot_general(a, b, dims, preferred_element_type=F32)


def kernel(
    q_ref, k_ref, v_ref, o_ref, do_ref, x_ref, w_ref, wt_ref,
    gi_ref, gw_ref,
    qb, dob, kb, vb, e_ref, dp_ref, bias, mx, lx, rx, delta, st_send, st_recv,
    dkv_send, dkv_recv, dkv_own, dqt, dq_send, dq_recv, g_ref,
    xa, xg, xt, wv, gwp, gwr, gip, gis, gia, gir,
    send, recv, local,
):
    t, c = lax.axis_index("tensor"), lax.axis_index("context")
    x, z = c // NZ, c % NZ
    y, k = t // NK, t % NK
    side = 2 * (c % 2) - 1
    partner = c - side
    near = (c + side + NC) % NC
    far = (c + 2 * side + NC) % NC
    far_user = (c - 2 * side + NC) % NC

    def x_peer(r):
        return (t, ((x + r) % NX) * NZ + z)

    def z_peer(r):
        return (t, x * NZ + (z + r) % NZ)

    def y_peer(r):
        return (((y + r) % NY) * NK + k, c)

    sibling = (y * NK + 1 - k, c)

    barrier = pltpu.get_barrier_semaphore()
    peers = [(t, near), (t, far), (t, far_user), sibling]
    peers += [x_peer(r) for r in range(1, NX)]
    peers += [z_peer(r) for r in range(1, NZ)]
    peers += [y_peer(r) for r in range(1, NY)]
    for peer in peers:
        pl.semaphore_signal(barrier, inc=1, device_id=peer, device_id_type=MESH)
    pl.semaphore_wait(barrier, len(peers))

    started = []

    def push(src, dst, device):
        number = len(started)
        copy = pltpu.make_async_remote_copy(
            src_ref=src,
            dst_ref=dst,
            send_sem=send.at[number],
            recv_sem=recv.at[number],
            device_id=device,
            device_id_type=MESH,
        )
        copy.start()
        started.append(copy)
        return copy

    to_partner = [
        push(q_ref, qb.at[pl.ds(ROWS, ROWS)], (t, partner)),
        push(do_ref, dob.at[pl.ds(ROWS, ROWS)], (t, partner)),
    ]
    to_near = [push(k_ref, kb.at[1], (t, near)), push(v_ref, vb.at[1], (t, near))]
    to_far = [push(k_ref, kb.at[2], (t, far_user)), push(v_ref, vb.at[2], (t, far_user))]
    x_first = [
        push(x_ref.at[:, :, pl.ds(((x + r) % NX) * DX, DX)], xa.at[x], x_peer(r))
        for r in range(1, NX)
    ]
    x_own = pltpu.make_async_copy(x_ref.at[:, :, pl.ds(x * DX, DX)], xa.at[x], local.at[0])
    x_own.start()
    w_copy = pltpu.make_async_copy(w_ref, wv, local.at[1])
    w_copy.start()

    qb[pl.ds(0, ROWS), :] = q_ref[...]
    dob[pl.ds(0, ROWS), :] = do_ref[...]
    kb[0] = k_ref[...]
    vb[0] = v_ref[...]

    window = wt_ref[...]
    first_tiles = [c * TILES, near * TILES, far * TILES]
    hits = [
        jnp.max(jnp.where(window == first + i, 1.0, 0.0), axis=0, keepdims=True)
        for first in first_tiles
        for i in range(TILES)
    ]
    hits = jnp.concatenate(hits + [jnp.zeros((4, NC * TILES), F32)], axis=0)
    column = lax.broadcasted_iota(jnp.int32, (NC * TILES, QUERIES), 1) // TILE
    entry = lax.broadcasted_iota(jnp.int32, (NC * TILES, QUERIES), 0)
    wanted = jnp.where(column < TILES, c * TILES + column, partner * TILES + column - TILES)
    pick = jnp.where(entry == wanted, 1.0, 0.0)
    bias[...] = (1.0 - dot(hits.astype(BF16), pick.astype(BF16), NN)) * MASKED

    st_send[...] = jnp.zeros_like(st_send)
    for h in range(HEADS):
        cols = pl.ds(h * HD, HD)
        product = do_ref[:, cols].astype(F32) * o_ref[:, cols].astype(F32)
        row = jnp.sum(product.T, axis=0, keepdims=True)
        delta[h, :, pl.ds(0, ROWS)] = row
        st_send[4 + h, :, pl.ds(0, ROWS)] = row

    def score_block(slot, first, count):
        def step(i, carry):
            h = i // count
            cols = pl.ds(pl.multiple_of((first + i % count) * CHUNK, CHUNK), CHUNK)
            head = pl.ds(pl.multiple_of(h * HD, HD), HD)
            s = dot(kb[slot, :, head], qb[cols, head], NTR) * (SCALE * LOG2E)
            parts = [
                s[i * TILE : (i + 1) * TILE] + bias[pl.ds(slot * TILES + i, 1), cols]
                for i in range(TILES)
            ]
            top = functools.reduce(jnp.maximum, parts)
            top = jnp.max(top, axis=0, keepdims=True)
            total = None
            for i, part in enumerate(parts):
                e = jnp.exp2(part - top)
                e_ref[h, pl.ds(slot * ROWS + i * TILE, TILE), cols] = e
                total = e if total is None else total + e
            mx[h * SLOTS + slot, :, cols] = top
            lx[h * SLOTS + slot, :, cols] = jnp.sum(total, axis=0, keepdims=True)
            return carry

        lax.fori_loop(0, HEADS * count, step, 0)

    def dprob_block(slot, first, count):
        def step(i, carry):
            h = i // count
            cols = pl.ds(pl.multiple_of((first + i % count) * CHUNK, CHUNK), CHUNK)
            head = pl.ds(pl.multiple_of(h * HD, HD), HD)
            dp_ref[h, pl.ds(slot * ROWS, ROWS), cols] = dot(vb[slot, :, head], dob[cols, head], NTR)
            return carry

        lax.fori_loop(0, HEADS * count, step, 0)

    half = ROWS // CHUNK
    score_block(0, 0, half)
    dprob_block(0, 0, half)

    x_own.wait()
    for copy in x_first:
        copy.wait_recv()
    x_second = [push(xa, xg.at[:, :, t], y_peer(r)) for r in range(1, NY)]
    x_side = [push(xa, xg.at[:, :, t], sibling)]
    x_place = pltpu.make_async_copy(xa, xg.at[:, :, t], local.at[2])
    x_place.start()

    for copy in to_partner:
        copy.wait_recv()
    score_block(0, half, half)
    dprob_block(0, half, half)
    for copy in to_near:
        copy.wait_recv()
    score_block(1, 0, 2 * half)
    dprob_block(1, 0, 2 * half)

    for r, copy in zip(range(1, NY), x_second):
        copy.wait_recv()
        origin = ((y - r + NY) % NY) * NK + k
        x_side.append(push(xg.at[:, :, origin], xg.at[:, :, origin], sibling))

    for copy in to_far:
        copy.wait_recv()
    score_block(2, 0, 2 * half)

    for h in range(HEADS):
        tops = [mx[h * SLOTS + j] for j in range(SLOTS)]
        top = functools.reduce(jnp.maximum, tops)
        total = sum(lx[h * SLOTS + j] * jnp.exp2(tops[j] - top) for j in range(SLOTS))
        st_send[h] = top
        st_send[2 + h] = total
    stats = push(st_send, st_recv, (t, partner))
    dprob_block(2, 0, 2 * half)
    stats.wait_recv()
    for h in range(HEADS):
        delta[h, :, pl.ds(ROWS, ROWS)] = st_recv[4 + h, :, pl.ds(0, ROWS)]
        for u in range(2):
            mine, theirs = pl.ds(u * ROWS, ROWS), pl.ds((1 - u) * ROWS, ROWS)
            top_a, top_b = st_send[h, :, mine], st_recv[h, :, theirs]
            top = jnp.maximum(top_a, top_b)
            total = st_send[2 + h, :, mine] * jnp.exp2(top_a - top)
            total = total + st_recv[2 + h, :, theirs] * jnp.exp2(top_b - top)
            lse = top + jnp.log2(total)
            for j in range(SLOTS):
                rx[h * SLOTS + j, :, mine] = jnp.exp2(mx[h * SLOTS + j, :, mine] - lse)

    dqt[...] = jnp.zeros_like(dqt)

    def grad_block(slot):
        def step(i, carry):
            h = i // 2
            part = pl.multiple_of((i % 2) * CHUNK, CHUNK)
            head = pl.ds(pl.multiple_of(h * HD, HD), HD)
            here = pl.ds(part, CHUNK)
            rows = pl.ds(slot * ROWS + part, CHUNK)
            keys_t = kb[slot, here, head].T
            grad_k = grad_v = None
            for u in range(2):
                cols = pl.ds(u * ROWS, ROWS)
                p = e_ref[h, rows, cols] * rx[h * SLOTS + slot, :, cols]
                ds = (p * (dp_ref[h, rows, cols] - delta[h, :, cols])).astype(BF16)
                dv = dot(p.astype(BF16), dob[cols, head], NN)
                dk = dot(ds, qb[cols, head], NN)
                grad_v = dv if grad_v is None else grad_v + dv
                grad_k = dk if grad_k is None else grad_k + dk
                dqt[h, :, cols] += dot(keys_t, ds, NN)
            if slot == 0:
                dkv_own[0, here, head] = grad_k * SCALE
                dkv_own[1, here, head] = grad_v
            else:
                dkv_send[2 * slot - 2, here, head] = (grad_k * SCALE).astype(BF16)
                dkv_send[2 * slot - 1, here, head] = grad_v.astype(BF16)
            return carry

        lax.fori_loop(0, HEADS * 2, step, 0)

    grad_block(2)
    returns = [push(dkv_send.at[2 + a], dkv_recv.at[2 + a], (t, far)) for a in range(2)]
    grad_block(1)
    returns += [push(dkv_send.at[a], dkv_recv.at[a], (t, near)) for a in range(2)]
    grad_block(0)
    for h in range(HEADS):
        dq_send[:, pl.ds(h * HD, HD)] = (dqt[h, :, pl.ds(ROWS, ROWS)] * SCALE).T.astype(BF16)
    dq_swap = push(dq_send, dq_recv, (t, partner))

    x_place.wait()
    for copy in x_side:
        copy.wait_recv()

    def turn(i, carry):
        for u in range(2):
            block = xg[i // 2, (i % 2) * 2 + u].reshape(TILE, DX)
            xt[:, pl.ds(pl.multiple_of(i * 2 * TILE, 2 * TILE) + u * TILE, TILE)] = block.T
        return carry

    lax.fori_loop(0, NX * TILES // 2, turn, 0)

    def gather(a):
        return [push(g_ref.at[a, x], g_ref.at[a, x], x_peer(r)) for r in range(1, NX)]

    def weight_share(a):
        def step(i, carry):
            rows = pl.ds(pl.multiple_of(i * 2 * DZ, 2 * DZ), 2 * DZ)
            part = dot(xt[rows, :], g_ref[a].reshape(NX * ROWS, WIDTH), NN)
            gwp[a, pl.ds(2 * i, 2)] = part.reshape(2, DZ, WIDTH).astype(BF16)
            return carry

        lax.fori_loop(0, NZ // 2, step, 0)
        return [push(gwp.at[a, (z + r) % NZ], gwr.at[a, z], z_peer(r)) for r in range(1, NZ)]

    dq_swap.wait_recv()
    for h in range(HEADS):
        cols = pl.ds(h * HD, HD)
        own = (dqt[h, :, pl.ds(0, ROWS)] * SCALE).T + dq_recv[:, cols].astype(F32)
        g_ref[0, x, :, :, :, :, cols] = own.astype(BF16).reshape(TILES, NY, NK, SHARE, HD)
    gathers = [gather(0)]
    for copy in gathers[0]:
        copy.wait_recv()
    shares = weight_share(0)

    for copy in returns:
        copy.wait_recv()
    for a in range(2):
        total = dkv_own[a] + dkv_recv[a].astype(F32) + dkv_recv[2 + a].astype(F32)
        g_ref[1 + a, x] = total.astype(BF16).reshape(TILES, NY, NK, SHARE, WIDTH)
        gathers.append(gather(1 + a))

    w_copy.wait()

    def input_share(core):
        def step(i, carry):
            cols = pl.ds(pl.multiple_of(i * 512, 512), 512)
            part = sum(
                dot(
                    g_ref[a, x, :, :, core].reshape(TILES * NY * SHARE, WIDTH),
                    wv[a, cols, :],
                    NTR,
                )
                for a in range(3)
            )
            gip[core, :, :, :, cols] = part.astype(BF16).reshape(TILES, NY, SHARE, 512)
            return carry

        lax.fori_loop(0, D // 512, step, 0)

    input_share(1 - k)
    cross = push(gip.at[1 - k], gis, sibling)
    input_share(k)

    for a in (1, 2):
        for copy in gathers[a]:
            copy.wait_recv()
        shares += weight_share(a)

    cross.wait_recv()

    def add_cores(i, carry):
        gia[i] = (gip[k, i].astype(F32) + gis[i].astype(F32)).astype(BF16)
        return carry

    lax.fori_loop(0, TILES, add_cores, 0)
    spread = [push(gia.at[:, (y + r) % NY], gir.at[r - 1], y_peer(r)) for r in range(1, NY)]

    for copy in shares:
        copy.wait_recv()
    for a in range(3):
        total = gwp[a, z].astype(F32)
        for r in range(1, NZ):
            total = total + gwr[a, (z + r) % NZ].astype(F32)
        gw_ref[a] = total

    for copy in spread:
        copy.wait_recv()

    def add_chips(i, carry):
        total = gia[i, y].astype(F32)
        for r in range(NY - 1):
            total = total + gir[r, i].astype(F32)
        gi_ref[i] = total.astype(BF16)
        return carry

    lax.fori_loop(0, TILES, add_chips, 0)

    for copy in started:
        copy.wait_send()


N_COPIES = 6 + 3 + 3 + 4 + 1 + 4 + 1 + 3 * (NX - 1) + 3 * (NZ - 1) + 1 + 3


def body(normed_input, w_qkv, queries, saved_keys, values, attn_out, grad_out, window_tiles):
    vmem = pl.BlockSpec(memory_space=pltpu.VMEM)
    anywhere = pl.BlockSpec(memory_space=pl.ANY)
    block = (ROWS, WIDTH)
    grads = (3, NX, TILES, NY, NK, SHARE, WIDTH)
    scratch = [
        ((QUERIES, WIDTH), BF16),
        ((QUERIES, WIDTH), BF16),
        ((SLOTS, *block), BF16),
        ((SLOTS, *block), BF16),
        ((HEADS, KEYS, QUERIES), F32),
        ((HEADS, KEYS, QUERIES), F32),
        ((16, QUERIES), F32),
        ((HEADS * SLOTS, 1, QUERIES), F32),
        ((HEADS * SLOTS, 1, QUERIES), F32),
        ((HEADS * SLOTS, 1, QUERIES), F32),
        ((HEADS, 1, QUERIES), F32),
        ((6, 1, QUERIES), F32),
        ((6, 1, QUERIES), F32),
        ((4, *block), BF16),
        ((4, *block), BF16),
        ((2, *block), F32),
        ((HEADS, HD, QUERIES), F32),
        (block, BF16),
        (block, BF16),
        (grads, BF16),
        ((NX, TILES, SHARE, DX), BF16),
        ((NX, TILES, NT, SHARE, DX), BF16),
        ((DX, NX * ROWS), BF16),
        ((3, D, WIDTH), BF16),
        ((3, NZ, DZ, WIDTH), BF16),
        ((3, NZ, DZ, WIDTH), BF16),
        ((NK, TILES, NY, SHARE, D), BF16),
        ((TILES, NY, SHARE, D), BF16),
        ((TILES, NY, SHARE, D), BF16),
        ((NY - 1, TILES, SHARE, D), BF16),
    ]
    grad_input, grad_w = pl.pallas_call(
        kernel,
        out_shape=[
            jax.ShapeDtypeStruct((TILES, SHARE, D), BF16),
            jax.ShapeDtypeStruct((3, DZ, WIDTH), F32),
        ],
        in_specs=[vmem] * 5 + [anywhere] * 2 + [vmem],
        out_specs=[vmem, vmem],
        scratch_shapes=[pltpu.VMEM(shape, kind) for shape, kind in scratch]
        + [
            pltpu.SemaphoreType.DMA((N_COPIES,)),
            pltpu.SemaphoreType.DMA((N_COPIES,)),
            pltpu.SemaphoreType.DMA((3,)),
        ],
        compiler_params=pltpu.CompilerParams(
            collective_id=0, has_side_effects=True, vmem_limit_bytes=60 * 2**20
        ),
        name="window_grads",
    )(
        queries,
        saved_keys,
        values,
        attn_out,
        grad_out,
        normed_input,
        w_qkv.transpose(1, 0, 2),
        window_tiles.T,
    )
    return grad_input, grad_w.transpose(1, 0, 2)


def solution(mesh):
    placed = (
        P("context", "tensor", None),
        P(None, None, "tensor"),
        P("context", "tensor"),
        P("context", "tensor"),
        P("context", "tensor"),
        P("context", "tensor"),
        P("context", "tensor"),
        P(),
    )
    return jax.shard_map(
        body,
        mesh=mesh,
        in_specs=placed,
        out_specs=(P("context", "tensor", None), P("context", None, "tensor")),
        check_vma=False,
    )
```

time: 657 us -> 152 us (0.23)
  the two profiles are of different devices: /device:TPU:2 before, /device:TPU:1 now
where the time goes in v1:
time: 152 us
  Pallas kernels  148 us (97%)
  local copies, waits for them, and re-layouts  3.46 us (2%)
    pallas_call x1, Pallas kernels, body(): pl.pallas_call(kernel, out_shape=[jax.ShapeDtypeStruct((TILES, SHARE, D),...  148 us
    unnamed x2, local copies, waits for them, and re-layouts  3.46 us

profile of v1, /device:TPU:1, one launch (start us, length us, event | category | flops | bytes accessed | tf_op | source)
XLA Modules:
  0.0 152.3 jit_solution(15988964938704348889)
XLA Ops:
  0.6 148.2 %window_grads.1 = (bf16[4,16,3072]{2,1,0:T(8,128)(2,1)}, f32[3,96,256]{2,1,0:T(8,128)}) custom-call(bf16[512,256]{1,0:T(8,128)(2,1)} %q_ref.1, bf16[512,256]{1,0:T(8,128)(2,1)} %k_ref.1, bf16[512,256]{1,0:T(8,128)(2,1)} %v_ref.1, bf16[512,256]{1,0:T(8,128)(2,1)} %o_ref.1, bf16[512,256]{1,0:T(8,128)(2,1)} %do_ref.1, bf16[4,16,3072]{2,1,0:T(8,128)(2,1)} %x_ref.1, ...), custom_call_target="tpu_custom_call" | custom-call | tf_op jit(solution)/shard_map/window_grads/pallas_call | solution.py:401
  148.8 1.8 %copy.12 = bf16[4,16,3072]{2,1,0:T(8,128)(2,1)} copy(bf16[4,16,3072]{2,1,0:T(8,128)(2,1)} %get-tuple-element.8) | data formatting | bytes 786432
  150.6 1.7 %copy.13 = f32[96,3,256]{2,0,1:T(8,128)} copy(f32[96,3,256]{2,0,1:T(8,128)} %bitcast.4) | data formatting | bytes 589824

commit v2 on v1

--- a/solution.py
+++ b/solution.py
@@ -41,9 +41,9 @@
 def kernel(
     q_ref, k_ref, v_ref, o_ref, do_ref, x_ref, w_ref, wt_ref,
     gi_ref, gw_ref,
-    qb, dob, kb, vb, e_ref, dp_ref, bias, mx, lx, rx, delta, st_send, st_recv,
+    qb, dob, kb, vb, e_ref, bias, mx, lx, rx, delta, st_send, st_recv,
     dkv_send, dkv_recv, dkv_own, dqt, dq_send, dq_recv, g_ref,
-    xa, xg, xt, wv, gwp, gwr, gip, gis, gia, gir,
+    xy, xg, xt, wv, gwp, gwr, gip, gis, gia, gir,
     send, recv, local,
 ):
     t, c = lax.axis_index("tensor"), lax.axis_index("context")
@@ -91,17 +91,13 @@
         started.append(copy)
         return copy
 
-    to_partner = [
-        push(q_ref, qb.at[pl.ds(ROWS, ROWS)], (t, partner)),
-        push(do_ref, dob.at[pl.ds(ROWS, ROWS)], (t, partner)),
-    ]
-    to_near = [push(k_ref, kb.at[1], (t, near)), push(v_ref, vb.at[1], (t, near))]
-    to_far = [push(k_ref, kb.at[2], (t, far_user)), push(v_ref, vb.at[2], (t, far_user))]
-    x_first = [
-        push(x_ref.at[:, :, pl.ds(((x + r) % NX) * DX, DX)], xa.at[x], x_peer(r))
-        for r in range(1, NX)
-    ]
-    x_own = pltpu.make_async_copy(x_ref.at[:, :, pl.ds(x * DX, DX)], xa.at[x], local.at[0])
+    x_first = [push(x_ref, xy.at[:, y], y_peer(r)) for r in range(1, NY)]
+    q_swap = push(q_ref, qb.at[pl.ds(ROWS, ROWS)], (t, partner))
+    k_near = push(k_ref, kb.at[1], (t, near))
+    k_far = push(k_ref, kb.at[2], (t, far_user))
+    do_swap = push(do_ref, dob.at[pl.ds(ROWS, ROWS)], (t, partner))
+    v_near = push(v_ref, vb.at[1], (t, near))
+    x_own = pltpu.make_async_copy(x_ref, xy.at[:, y], local.at[0])
     x_own.start()
     w_copy = pltpu.make_async_copy(w_ref, wv, local.at[1])
     w_copy.start()
@@ -156,44 +152,13 @@
 
         lax.fori_loop(0, HEADS * count, step, 0)
 
-    def dprob_block(slot, first, count):
-        def step(i, carry):
-            h = i // count
-            cols = pl.ds(pl.multiple_of((first + i % count) * CHUNK, CHUNK), CHUNK)
-            head = pl.ds(pl.multiple_of(h * HD, HD), HD)
-            dp_ref[h, pl.ds(slot * ROWS, ROWS), cols] = dot(vb[slot, :, head], dob[cols, head], NTR)
-            return carry
-
-        lax.fori_loop(0, HEADS * count, step, 0)
-
     half = ROWS // CHUNK
     score_block(0, 0, half)
-    dprob_block(0, 0, half)
-
-    x_own.wait()
-    for copy in x_first:
-        copy.wait_recv()
-    x_second = [push(xa, xg.at[:, :, t], y_peer(r)) for r in range(1, NY)]
-    x_side = [push(xa, xg.at[:, :, t], sibling)]
-    x_place = pltpu.make_async_copy(xa, xg.at[:, :, t], local.at[2])
-    x_place.start()
-
-    for copy in to_partner:
-        copy.wait_recv()
+    q_swap.wait_recv()
     score_block(0, half, half)
-    dprob_block(0, half, half)
-    for copy in to_near:
-        copy.wait_recv()
+    k_near.wait_recv()
     score_block(1, 0, 2 * half)
-    dprob_block(1, 0, 2 * half)
-
-    for r, copy in zip(range(1, NY), x_second):
-        copy.wait_recv()
-        origin = ((y - r + NY) % NY) * NK + k
-        x_side.append(push(xg.at[:, :, origin], xg.at[:, :, origin], sibling))
-
-    for copy in to_far:
-        copy.wait_recv()
+    k_far.wait_recv()
     score_block(2, 0, 2 * half)
 
     for h in range(HEADS):
@@ -203,7 +168,8 @@
         st_send[h] = top
         st_send[2 + h] = total
     stats = push(st_send, st_recv, (t, partner))
-    dprob_block(2, 0, 2 * half)
+    v_far = push(v_ref, vb.at[2], (t, far_user))
+    dqt[...] = jnp.zeros_like(dqt)
     stats.wait_recv()
     for h in range(HEADS):
         delta[h, :, pl.ds(ROWS, ROWS)] = st_recv[4 + h, :, pl.ds(0, ROWS)]
@@ -217,8 +183,6 @@
             for j in range(SLOTS):
                 rx[h * SLOTS + j, :, mine] = jnp.exp2(mx[h * SLOTS + j, :, mine] - lse)
 
-    dqt[...] = jnp.zeros_like(dqt)
-
     def grad_block(slot):
         def step(i, carry):
             h = i // 2
@@ -227,11 +191,13 @@
             here = pl.ds(part, CHUNK)
             rows = pl.ds(slot * ROWS + part, CHUNK)
             keys_t = kb[slot, here, head].T
+            value = vb[slot, here, head]
             grad_k = grad_v = None
             for u in range(2):
                 cols = pl.ds(u * ROWS, ROWS)
                 p = e_ref[h, rows, cols] * rx[h * SLOTS + slot, :, cols]
-                ds = (p * (dp_ref[h, rows, cols] - delta[h, :, cols])).astype(BF16)
+                dp = dot(value, dob[cols, head], NTR)
+                ds = (p * (dp - delta[h, :, cols])).astype(BF16)
                 dv = dot(p.astype(BF16), dob[cols, head], NN)
                 dk = dot(ds, qb[cols, head], NN)
                 grad_v = dv if grad_v is None else grad_v + dv
@@ -247,18 +213,39 @@
 
         lax.fori_loop(0, HEADS * 2, step, 0)
 
+    do_swap.wait_recv()
+    v_near.wait_recv()
+    grad_block(1)
+    dv_near = push(dkv_send.at[1], dkv_recv.at[1], (t, near))
+    dk_near = push(dkv_send.at[0], dkv_recv.at[0], (t, near))
+
+    x_own.wait()
+    for copy in x_first:
+        copy.wait_recv()
+    x_second = [
+        push(
+            xy.at[:, :, :, pl.ds(((x + r) % NX) * DX, DX)], xg.at[x, :, :, k], x_peer(r)
+        )
+        for r in range(1, NX)
+    ]
+    x_place = pltpu.make_async_copy(
+        xy.at[:, :, :, pl.ds(x * DX, DX)], xg.at[x, :, :, k], local.at[2]
+    )
+    x_place.start()
+
+    v_far.wait_recv()
     grad_block(2)
-    returns = [push(dkv_send.at[2 + a], dkv_recv.at[2 + a], (t, far)) for a in range(2)]
-    grad_block(1)
-    returns += [push(dkv_send.at[a], dkv_recv.at[a], (t, near)) for a in range(2)]
+    dv_far = push(dkv_send.at[3], dkv_recv.at[3], (t, far))
+    dk_far = push(dkv_send.at[2], dkv_recv.at[2], (t, far))
     grad_block(0)
     for h in range(HEADS):
         dq_send[:, pl.ds(h * HD, HD)] = (dqt[h, :, pl.ds(ROWS, ROWS)] * SCALE).T.astype(BF16)
     dq_swap = push(dq_send, dq_recv, (t, partner))
 
     x_place.wait()
-    for copy in x_side:
-        copy.wait_recv()
+    for copy in x_second:
+        copy.wait_recv()
+    x_side = push(xg.at[:, :, :, k], xg.at[:, :, :, k], sibling)
 
     def turn(i, carry):
         for u in range(2):
@@ -266,10 +253,16 @@
             xt[:, pl.ds(pl.multiple_of(i * 2 * TILE, 2 * TILE) + u * TILE, TILE)] = block.T
         return carry
 
-    lax.fori_loop(0, NX * TILES // 2, turn, 0)
-
     def gather(a):
-        return [push(g_ref.at[a, x], g_ref.at[a, x], x_peer(r)) for r in range(1, NX)]
+        return [push(g_ref.at[a, x], g_ref.at[a, x], x_peer(r)) for r in (1, NX - 1)]
+
+    def gather_on(a, first):
+        copies = []
+        for copy, r, part in zip(first, (1, NX - 1), (0, TILES // 2)):
+            copy.wait_recv()
+            piece = g_ref.at[a, (x - r + NX) % NX, pl.ds(part, TILES // 2)]
+            copies.append(push(piece, piece, x_peer(r)))
+        return copies
 
     def weight_share(a):
         def step(i, carry):
@@ -281,22 +274,28 @@
         lax.fori_loop(0, NZ // 2, step, 0)
         return [push(gwp.at[a, (z + r) % NZ], gwr.at[a, z], z_peer(r)) for r in range(1, NZ)]
 
+    def join(a):
+        total = dkv_own[a] + dkv_recv[a].astype(F32) + dkv_recv[2 + a].astype(F32)
+        g_ref[1 + a, x] = total.astype(BF16).reshape(TILES, NY, NK, SHARE, WIDTH)
+
     dq_swap.wait_recv()
     for h in range(HEADS):
         cols = pl.ds(h * HD, HD)
         own = (dqt[h, :, pl.ds(0, ROWS)] * SCALE).T + dq_recv[:, cols].astype(F32)
         g_ref[0, x, :, :, :, :, cols] = own.astype(BF16).reshape(TILES, NY, NK, SHARE, HD)
-    gathers = [gather(0)]
-    for copy in gathers[0]:
-        copy.wait_recv()
-    shares = weight_share(0)
-
-    for copy in returns:
-        copy.wait_recv()
-    for a in range(2):
-        total = dkv_own[a] + dkv_recv[a].astype(F32) + dkv_recv[2 + a].astype(F32)
-        g_ref[1 + a, x] = total.astype(BF16).reshape(TILES, NY, NK, SHARE, WIDTH)
-        gathers.append(gather(1 + a))
+    q_first = gather(0)
+    dv_near.wait_recv()
+    dv_far.wait_recv()
+    join(1)
+    v_first = gather(2)
+    x_side.wait_recv()
+    lax.fori_loop(0, NX * TILES // 2, turn, 0)
+    q_last = gather_on(0, q_first)
+    dk_near.wait_recv()
+    dk_far.wait_recv()
+    join(0)
+    k_first = gather(1)
+    v_last = gather_on(2, v_first)
 
     w_copy.wait()
 
@@ -318,12 +317,14 @@
 
     input_share(1 - k)
     cross = push(gip.at[1 - k], gis, sibling)
+    for copy in q_last:
+        copy.wait_recv()
+    shares = weight_share(0)
+    k_last = gather_on(1, k_first)
     input_share(k)
-
-    for a in (1, 2):
-        for copy in gathers[a]:
-            copy.wait_recv()
-        shares += weight_share(a)
+    for copy in v_last:
+        copy.wait_recv()
+    shares += weight_share(2)
 
     cross.wait_recv()
 
@@ -333,6 +334,9 @@
 
     lax.fori_loop(0, TILES, add_cores, 0)
     spread = [push(gia.at[:, (y + r) % NY], gir.at[r - 1], y_peer(r)) for r in range(1, NY)]
+    for copy in k_last:
+        copy.wait_recv()
+    shares += weight_share(1)
 
     for copy in shares:
         copy.wait_recv()
@@ -358,7 +362,7 @@
         copy.wait_send()
 
 
-N_COPIES = 6 + 3 + 3 + 4 + 1 + 4 + 1 + 3 * (NX - 1) + 3 * (NZ - 1) + 1 + 3
+N_COPIES = 6 + 3 + 3 + 1 + 1 + 4 + 1 + 3 * 4 + 3 * (NZ - 1) + 1 + 3
 
 
 def body(normed_input, w_qkv, queries, saved_keys, values, attn_out, grad_out, window_tiles):
@@ -371,7 +375,6 @@
         ((QUERIES, WIDTH), BF16),
         ((SLOTS, *block), BF16),
         ((SLOTS, *block), BF16),
-        ((HEADS, KEYS, QUERIES), F32),
         ((HEADS, KEYS, QUERIES), F32),
         ((16, QUERIES), F32),
         ((HEADS * SLOTS, 1, QUERIES), F32),
@@ -387,8 +390,8 @@
         (block, BF16),
         (block, BF16),
         (grads, BF16),
-        ((NX, TILES, SHARE, DX), BF16),
-        ((NX, TILES, NT, SHARE, DX), BF16),
+        ((TILES, NY, SHARE, D), BF16),
+        ((NX, TILES, NY, NK, SHARE, DX), BF16),
         ((DX, NX * ROWS), BF16),
         ((3, D, WIDTH), BF16),
         ((3, NZ, DZ, WIDTH), BF16),

time: 152 us -> 116 us (0.76)
  the two profiles are of different devices: /device:TPU:1 before, /device:TPU:2 now
where the time goes in v2:
time: 116 us
  Pallas kernels  112 us (97%)
  local copies, waits for them, and re-layouts  3.46 us (3%)
    pallas_call x1, Pallas kernels, body(): pl.pallas_call(kernel, out_shape=[jax.ShapeDtypeStruct((TILES, SHARE, D),...  112 us
    unnamed x2, local copies, waits for them, and re-layouts  3.46 us

profile of v2, /device:TPU:2, one launch (start us, length us, event | category | flops | bytes accessed | tf_op | source)
XLA Modules:
  0.0 115.8 jit_solution(11641486411273759220)
XLA Ops:
  0.6 111.7 %window_grads.1 = (bf16[4,16,3072]{2,1,0:T(8,128)(2,1)}, f32[3,96,256]{2,1,0:T(8,128)}) custom-call(bf16[512,256]{1,0:T(8,128)(2,1)} %q_ref.1, bf16[512,256]{1,0:T(8,128)(2,1)} %k_ref.1, bf16[512,256]{1,0:T(8,128)(2,1)} %v_ref.1, bf16[512,256]{1,0:T(8,128)(2,1)} %o_ref.1, bf16[512,256]{1,0:T(8,128)(2,1)} %do_ref.1, bf16[4,16,3072]{2,1,0:T(8,128)(2,1)} %x_ref.1, ...), custom_call_target="tpu_custom_call" | custom-call | tf_op jit(solution)/shard_map/window_grads/pallas_call | solution.py:404
  112.4 1.8 %copy.12 = bf16[4,16,3072]{2,1,0:T(8,128)(2,1)} copy(bf16[4,16,3072]{2,1,0:T(8,128)(2,1)} %get-tuple-element.8) | data formatting | bytes 786432
  114.1 1.7 %copy.13 = f32[96,3,256]{2,0,1:T(8,128)} copy(f32[96,3,256]{2,0,1:T(8,128)} %bitcast.4) | data formatting | bytes 589824

commit v3 on v2

--- a/solution.py
+++ b/solution.py
@@ -43,7 +43,7 @@
     gi_ref, gw_ref,
     qb, dob, kb, vb, e_ref, bias, mx, lx, rx, delta, st_send, st_recv,
     dkv_send, dkv_recv, dkv_own, dqt, dq_send, dq_recv, g_ref,
-    xy, xg, xt, wv, gwp, gwr, gip, gis, gia, gir,
+    xa, xg, xt, wv, gwp, gwr, gip, gis, gia, gib, gir,
     send, recv, local,
 ):
     t, c = lax.axis_index("tensor"), lax.axis_index("context")
@@ -91,13 +91,13 @@
         started.append(copy)
         return copy
 
-    x_first = [push(x_ref, xy.at[:, y], y_peer(r)) for r in range(1, NY)]
+    x_first = [
+        push(x_ref.at[:, :, pl.ds(((x + r) % NX) * DX, DX)], xa.at[x], x_peer(r))
+        for r in range(1, NX)
+    ]
     q_swap = push(q_ref, qb.at[pl.ds(ROWS, ROWS)], (t, partner))
-    k_near = push(k_ref, kb.at[1], (t, near))
-    k_far = push(k_ref, kb.at[2], (t, far_user))
     do_swap = push(do_ref, dob.at[pl.ds(ROWS, ROWS)], (t, partner))
-    v_near = push(v_ref, vb.at[1], (t, near))
-    x_own = pltpu.make_async_copy(x_ref, xy.at[:, y], local.at[0])
+    x_own = pltpu.make_async_copy(x_ref.at[:, :, pl.ds(x * DX, DX)], xa.at[x], local.at[0])
     x_own.start()
     w_copy = pltpu.make_async_copy(w_ref, wv, local.at[1])
     w_copy.start()
@@ -152,8 +152,19 @@
 
         lax.fori_loop(0, HEADS * count, step, 0)
 
+    x_own.wait()
+    for copy in x_first:
+        copy.wait_recv()
+    k_near = push(k_ref, kb.at[1], (t, near))
+    k_far = push(k_ref, kb.at[2], (t, far_user))
+    v_near = push(v_ref, vb.at[1], (t, near))
+    x_second = [push(xa, xg.at[:, :, y, k], y_peer(r)) for r in range(1, NY)]
+    x_place = pltpu.make_async_copy(xa, xg.at[:, :, y, k], local.at[2])
+    x_place.start()
+
     half = ROWS // CHUNK
     score_block(0, 0, half)
+
     q_swap.wait_recv()
     score_block(0, half, half)
     k_near.wait_recv()
@@ -170,6 +181,7 @@
     stats = push(st_send, st_recv, (t, partner))
     v_far = push(v_ref, vb.at[2], (t, far_user))
     dqt[...] = jnp.zeros_like(dqt)
+
     stats.wait_recv()
     for h in range(HEADS):
         delta[h, :, pl.ds(ROWS, ROWS)] = st_recv[4 + h, :, pl.ds(0, ROWS)]
@@ -219,20 +231,6 @@
     dv_near = push(dkv_send.at[1], dkv_recv.at[1], (t, near))
     dk_near = push(dkv_send.at[0], dkv_recv.at[0], (t, near))
 
-    x_own.wait()
-    for copy in x_first:
-        copy.wait_recv()
-    x_second = [
-        push(
-            xy.at[:, :, :, pl.ds(((x + r) % NX) * DX, DX)], xg.at[x, :, :, k], x_peer(r)
-        )
-        for r in range(1, NX)
-    ]
-    x_place = pltpu.make_async_copy(
-        xy.at[:, :, :, pl.ds(x * DX, DX)], xg.at[x, :, :, k], local.at[2]
-    )
-    x_place.start()
-
     v_far.wait_recv()
     grad_block(2)
     dv_far = push(dkv_send.at[3], dkv_recv.at[3], (t, far))
@@ -242,11 +240,6 @@
         dq_send[:, pl.ds(h * HD, HD)] = (dqt[h, :, pl.ds(ROWS, ROWS)] * SCALE).T.astype(BF16)
     dq_swap = push(dq_send, dq_recv, (t, partner))
 
-    x_place.wait()
-    for copy in x_second:
-        copy.wait_recv()
-    x_side = push(xg.at[:, :, :, k], xg.at[:, :, :, k], sibling)
-
     def turn(i, carry):
         for u in range(2):
             block = xg[i // 2, (i % 2) * 2 + u].reshape(TILE, DX)
@@ -284,6 +277,12 @@
         own = (dqt[h, :, pl.ds(0, ROWS)] * SCALE).T + dq_recv[:, cols].astype(F32)
         g_ref[0, x, :, :, :, :, cols] = own.astype(BF16).reshape(TILES, NY, NK, SHARE, HD)
     q_first = gather(0)
+
+    x_place.wait()
+    for copy in x_second:
+        copy.wait_recv()
+    x_side = push(xg.at[:, :, :, k], xg.at[:, :, :, k], sibling)
+
     dv_near.wait_recv()
     dv_far.wait_recv()
     join(1)
@@ -295,14 +294,14 @@
     dk_far.wait_recv()
     join(0)
     k_first = gather(1)
-    v_last = gather_on(2, v_first)
 
     w_copy.wait()
-
-    def input_share(core):
+    part_cols = [pl.ds(i * (D // 2), D // 2) for i in range(2)]
+
+    def input_share(core, part):
         def step(i, carry):
-            cols = pl.ds(pl.multiple_of(i * 512, 512), 512)
-            part = sum(
+            cols = pl.ds(pl.multiple_of(part * (D // 2) + i * 512, 512), 512)
+            total = sum(
                 dot(
                     g_ref[a, x, :, :, core].reshape(TILES * NY * SHARE, WIDTH),
                     wv[a, cols, :],
@@ -310,30 +309,49 @@
                 )
                 for a in range(3)
             )
-            gip[core, :, :, :, cols] = part.astype(BF16).reshape(TILES, NY, SHARE, 512)
+            gip[core, :, :, :, cols] = total.astype(BF16).reshape(TILES, NY, SHARE, 512)
             return carry
 
-        lax.fori_loop(0, D // 512, step, 0)
-
-    input_share(1 - k)
-    cross = push(gip.at[1 - k], gis, sibling)
+        lax.fori_loop(0, D // 1024, step, 0)
+
+    cross = []
+    for i, cols in enumerate(part_cols):
+        input_share(1 - k, i)
+        cross.append(push(gip.at[1 - k, :, :, :, cols], gis.at[:, :, :, cols], sibling))
     for copy in q_last:
         copy.wait_recv()
     shares = weight_share(0)
+    v_last = gather_on(2, v_first)
+    for i in range(2):
+        input_share(k, i)
+
+    up, down = (y + 1) % NY, (y + NY - 1) % NY
+    ahead, early, late = [], [], []
+    for i, cols in enumerate(part_cols):
+        cross[i].wait_recv()
+
+        def add_cores(j, carry):
+            both = gip[k, j, :, :, cols].astype(F32) + gis[j, :, :, cols].astype(F32)
+            gia[j, :, :, cols] = both.astype(BF16)
+            return carry
+
+        lax.fori_loop(0, TILES, add_cores, 0)
+        forth, back = (y_peer(1), y_peer(NY - 1)) if i == 0 else (y_peer(NY - 1), y_peer(1))
+        near_by = down if i == 0 else up
+        ahead.append(push(gia.at[:, (y + 2) % NY, :, cols], gib.at[i], forth))
+        early.append(push(gia.at[:, near_by, :, cols], gir.at[1 - i, :, :, cols], back))
+
     k_last = gather_on(1, k_first)
-    input_share(k)
     for copy in v_last:
         copy.wait_recv()
     shares += weight_share(2)
-
-    cross.wait_recv()
-
-    def add_cores(i, carry):
-        gia[i] = (gip[k, i].astype(F32) + gis[i].astype(F32)).astype(BF16)
-        return carry
-
-    lax.fori_loop(0, TILES, add_cores, 0)
-    spread = [push(gia.at[:, (y + r) % NY], gir.at[r - 1], y_peer(r)) for r in range(1, NY)]
+    for i, cols in enumerate(part_cols):
+        ahead[i].wait_recv()
+        near_by = up if i == 0 else down
+        through = gia[:, near_by, :, cols].astype(F32) + gib[i].astype(F32)
+        gia[:, near_by, :, cols] = through.astype(BF16)
+        forth = y_peer(1) if i == 0 else y_peer(NY - 1)
+        late.append(push(gia.at[:, near_by, :, cols], gir.at[i, :, :, cols], forth))
     for copy in k_last:
         copy.wait_recv()
     shares += weight_share(1)
@@ -346,12 +364,12 @@
             total = total + gwr[a, (z + r) % NZ].astype(F32)
         gw_ref[a] = total
 
-    for copy in spread:
+    for copy in early + late:
         copy.wait_recv()
 
     def add_chips(i, carry):
         total = gia[i, y].astype(F32)
-        for r in range(NY - 1):
+        for r in range(2):
             total = total + gir[r, i].astype(F32)
         gi_ref[i] = total.astype(BF16)
         return carry
@@ -362,7 +380,7 @@
         copy.wait_send()
 
 
-N_COPIES = 6 + 3 + 3 + 1 + 1 + 4 + 1 + 3 * 4 + 3 * (NZ - 1) + 1 + 3
+N_COPIES = 6 + 3 + 3 + 1 + 1 + 4 + 1 + 3 * 4 + 3 * (NZ - 1) + 2 + 6
 
 
 def body(normed_input, w_qkv, queries, saved_keys, values, attn_out, grad_out, window_tiles):
@@ -390,7 +408,7 @@
         (block, BF16),
         (block, BF16),
         (grads, BF16),
-        ((TILES, NY, SHARE, D), BF16),
+        ((NX, TILES, SHARE, DX), BF16),
         ((NX, TILES, NY, NK, SHARE, DX), BF16),
         ((DX, NX * ROWS), BF16),
         ((3, D, WIDTH), BF16),
@@ -399,7 +417,8 @@
         ((NK, TILES, NY, SHARE, D), BF16),
         ((TILES, NY, SHARE, D), BF16),
         ((TILES, NY, SHARE, D), BF16),
-        ((NY - 1, TILES, SHARE, D), BF16),
+        ((2, TILES, SHARE, D // 2), BF16),
+        ((2, TILES, SHARE, D), BF16),
     ]
     grad_input, grad_w = pl.pallas_call(
         kernel,
@@ -407,7 +426,7 @@
             jax.ShapeDtypeStruct((TILES, SHARE, D), BF16),
             jax.ShapeDtypeStruct((3, DZ, WIDTH), F32),
         ],
-        in_specs=[vmem] * 5 + [anywhere] * 2 + [vmem],
+        in_specs=[vmem] * 6 + [anywhere, vmem],
         out_specs=[vmem, vmem],
         scratch_shapes=[pltpu.VMEM(shape, kind) for shape, kind in scratch]
         + [

time: 116 us -> 113 us (0.974)
  Pallas kernels: 112 us -> 108 us
    pallas_call x1, Pallas kernels: 112 us -> 108 us  [body(): pl.pallas_call(kernel, out_shape=[jax.ShapeDtypeStruct((TILES, SHARE, D),...]
where the time goes in v3:
time: 113 us; the launch traced here: 112 us
  Pallas kernels  108 us (96%)
  local copies, waits for them, and re-layouts  3.46 us (3%)
    pallas_call x1, Pallas kernels, body(): pl.pallas_call(kernel, out_shape=[jax.ShapeDtypeStruct((TILES, SHARE, D),...  108 us
    unnamed x2, local copies, waits for them, and re-layouts  3.46 us

profile of v3, /device:TPU:2, one launch (start us, length us, event | category | flops | bytes accessed | tf_op | source)
XLA Modules:
  0.0 112.4 jit_solution(5615236794941507812)
XLA Ops:
  0.6 108.3 %window_grads.1 = (bf16[4,16,3072]{2,1,0:T(8,128)(2,1)}, f32[3,96,256]{2,1,0:T(8,128)}) custom-call(bf16[512,256]{1,0:T(8,128)(2,1)} %q_ref.1, bf16[512,256]{1,0:T(8,128)(2,1)} %k_ref.1, bf16[512,256]{1,0:T(8,128)(2,1)} %v_ref.1, bf16[512,256]{1,0:T(8,128)(2,1)} %o_ref.1, bf16[512,256]{1,0:T(8,128)(2,1)} %do_ref.1, bf16[4,16,3072]{2,1,0:T(8,128)(2,1)} %x_ref.1, ...), custom_call_target="tpu_custom_call" | custom-call | tf_op jit(solution)/shard_map/window_grads/pallas_call | solution.py:423
  108.9 1.8 %copy.12 = bf16[4,16,3072]{2,1,0:T(8,128)(2,1)} copy(bf16[4,16,3072]{2,1,0:T(8,128)(2,1)} %get-tuple-element.8) | data formatting | bytes 786432
  110.7 1.7 %copy.13 = f32[96,3,256]{2,0,1:T(8,128)} copy(f32[96,3,256]{2,0,1:T(8,128)} %bitcast.4) | data formatting | bytes 589824

commit v4 on v3

--- a/solution.py
+++ b/solution.py
@@ -234,7 +234,6 @@
     v_far.wait_recv()
     grad_block(2)
     dv_far = push(dkv_send.at[3], dkv_recv.at[3], (t, far))
-    dk_far = push(dkv_send.at[2], dkv_recv.at[2], (t, far))
     grad_block(0)
     for h in range(HEADS):
         dq_send[:, pl.ds(h * HD, HD)] = (dqt[h, :, pl.ds(ROWS, ROWS)] * SCALE).T.astype(BF16)
@@ -287,6 +286,7 @@
     dv_far.wait_recv()
     join(1)
     v_first = gather(2)
+    dk_far = push(dkv_send.at[2], dkv_recv.at[2], (t, far))
     x_side.wait_recv()
     lax.fori_loop(0, NX * TILES // 2, turn, 0)
     q_last = gather_on(0, q_first)

time: 113 us -> 111 us (0.982)
    pallas_call x1, Pallas kernels: 108 us -> 107 us  [body(): pl.pallas_call(kernel, out_shape=[jax.ShapeDtypeStruct((TILES, SHARE, D),...]
where the time goes in v4:
time: 111 us
  Pallas kernels  107 us (96%)
  local copies, waits for them, and re-layouts  3.46 us (3%)
    pallas_call x1, Pallas kernels, body(): pl.pallas_call(kernel, out_shape=[jax.ShapeDtypeStruct((TILES, SHARE, D),...  107 us
    unnamed x2, local copies, waits for them, and re-layouts  3.46 us

profile of v4, /device:TPU:2, one launch (start us, length us, event | category | flops | bytes accessed | tf_op | source)
XLA Modules:
  0.0 110.8 jit_solution(2243922359919060340)
XLA Ops:
  0.6 106.7 %window_grads.1 = (bf16[4,16,3072]{2,1,0:T(8,128)(2,1)}, f32[3,96,256]{2,1,0:T(8,128)}) custom-call(bf16[512,256]{1,0:T(8,128)(2,1)} %q_ref.1, bf16[512,256]{1,0:T(8,128)(2,1)} %k_ref.1, bf16[512,256]{1,0:T(8,128)(2,1)} %v_ref.1, bf16[512,256]{1,0:T(8,128)(2,1)} %o_ref.1, bf16[512,256]{1,0:T(8,128)(2,1)} %do_ref.1, bf16[4,16,3072]{2,1,0:T(8,128)(2,1)} %x_ref.1, ...), custom_call_target="tpu_custom_call" | custom-call | tf_op jit(solution)/shard_map/window_grads/pallas_call | solution.py:423
  107.3 1.8 %copy.12 = bf16[4,16,3072]{2,1,0:T(8,128)(2,1)} copy(bf16[4,16,3072]{2,1,0:T(8,128)(2,1)} %get-tuple-element.8) | data formatting | bytes 786432
  109.1 1.7 %copy.13 = f32[96,3,256]{2,0,1:T(8,128)} copy(f32[96,3,256]{2,0,1:T(8,128)} %bitcast.4) | data formatting | bytes 589824

commit v5 on v4

--- a/solution.py
+++ b/solution.py
@@ -229,11 +229,11 @@
     v_near.wait_recv()
     grad_block(1)
     dv_near = push(dkv_send.at[1], dkv_recv.at[1], (t, near))
-    dk_near = push(dkv_send.at[0], dkv_recv.at[0], (t, near))
 
     v_far.wait_recv()
     grad_block(2)
     dv_far = push(dkv_send.at[3], dkv_recv.at[3], (t, far))
+    dk_near = push(dkv_send.at[0], dkv_recv.at[0], (t, near))
     grad_block(0)
     for h in range(HEADS):
         dq_send[:, pl.ds(h * HD, HD)] = (dqt[h, :, pl.ds(ROWS, ROWS)] * SCALE).T.astype(BF16)

time: 111 us -> 109 us (0.982)
  Pallas kernels: 107 us -> 104 us
    pallas_call x1, Pallas kernels: 107 us -> 104 us  [body(): pl.pallas_call(kernel, out_shape=[jax.ShapeDtypeStruct((TILES, SHARE, D),...]
where the time goes in v5:
time: 109 us; the launch traced here: 108 us
  Pallas kernels  104 us (95%)
  local copies, waits for them, and re-layouts  3.46 us (3%)
    pallas_call x1, Pallas kernels, body(): pl.pallas_call(kernel, out_shape=[jax.ShapeDtypeStruct((TILES, SHARE, D),...  104 us
    unnamed x2, local copies, waits for them, and re-layouts  3.46 us

profile of v5, /device:TPU:2, one launch (start us, length us, event | category | flops | bytes accessed | tf_op | source)
XLA Modules:
  0.0 107.9 jit_solution(15088999115737873462)
XLA Ops:
  0.6 103.8 %window_grads.1 = (bf16[4,16,3072]{2,1,0:T(8,128)(2,1)}, f32[3,96,256]{2,1,0:T(8,128)}) custom-call(bf16[512,256]{1,0:T(8,128)(2,1)} %q_ref.1, bf16[512,256]{1,0:T(8,128)(2,1)} %k_ref.1, bf16[512,256]{1,0:T(8,128)(2,1)} %v_ref.1, bf16[512,256]{1,0:T(8,128)(2,1)} %o_ref.1, bf16[512,256]{1,0:T(8,128)(2,1)} %do_ref.1, bf16[4,16,3072]{2,1,0:T(8,128)(2,1)} %x_ref.1, ...), custom_call_target="tpu_custom_call" | custom-call | tf_op jit(solution)/shard_map/window_grads/pallas_call | solution.py:423
  104.4 1.8 %copy.12 = bf16[4,16,3072]{2,1,0:T(8,128)(2,1)} copy(bf16[4,16,3072]{2,1,0:T(8,128)(2,1)} %get-tuple-element.8) | data formatting | bytes 786432
  106.2 1.7 %copy.13 = f32[96,3,256]{2,0,1:T(8,128)} copy(f32[96,3,256]{2,0,1:T(8,128)} %bitcast.4) | data formatting | bytes 589824
